TPU v7x, 128 devices: a whole 4x4x4 slice. The times are simulated.
128 devices in a mesh: ctx: 16 (over x, z_lo, core), vocab: 8 (over y, z_hi).
Axes of the slice: x: 4, y: 4, z: 4 (z_hi: 2, z_lo: 2; z = z_hi * 2 + z_lo), core: 2. Of those that a mesh axis runs over, the one named last changes fastest.
Arguments:
- hidden: bfloat16 [2048, 6144], P('ctx'), may hold values from -16 to 16
- labels: int32 [2048], P('ctx'), may hold values from 0 to 65535
- head_weight: bfloat16 [6144, 65536], P(None, ('ctx', 'vocab')), may hold values from -0.31894398 to 0.31894398
Outputs:
- token_loss: float32 [2048], P('ctx')
- head_grad: float32 [6144, 65536], P(None, ('ctx', 'vocab'))
All inputs are finite; a program needn't handle non-finite values.
Results may differ from a plain program's by a relative error of at most 0.0021.
Values may be sent and summed in bfloat16 or wider, within the bound.
A program may use at most 128 MiB of HBM per device.

v0:
```python
import heapq
import jax
import jax.numpy as jnp
from jax import lax
from jax.experimental import pallas as pl
from jax.experimental.pallas import tpu as pltpu
from jax.sharding import PartitionSpec as P

MESH = pl.DeviceIdType.MESH
z_weight = 0.0001

TOKENS_OF = (32, 64, 32)
SIZES = ((4, 5, 6, 5, 4), (5, 5, 4, 5, 5), (5, 5, 4, 5, 5))
REGIONS = ("F", "F'", "C", "S'", "S")
BLOCKS = ("0", "R", "2", "L")
LINKS = ("x+", "x-", "z+", "z-", "y+", "y-")
ORDER = {"x": ("F", "F'", "C", "S'"), "z": ("F", "F'", "C"), "y": ("F", "F'")}
NEAR = {"0": 0, "L": 1, "R": 1, "2": 2}
LANES = 128
N_CTX, N_VOCAB, N_X = 16, 8, 4


def onward(key):
    _, block, region, part = key
    links = []
    if block[0] != "Z":
        if region != "S":
            if block == "0":
                links += ["x+", "x-"]
            if (block, part) == ("L", 0):
                links.append("x+")
            if (block, part) == ("R", 1):
                links.append("x-")
        if region in ORDER["z"]:
            links.append(("z+", "z-")[part])
        if region == "F" and block != "0":
            links.append(("y+", "y-")[part])
    elif region in ORDER["y"]:
        links.append(("y+", "y-")[part])
    return links


def landing(link, key):
    phase, block, region, part = key
    if link[0] == "x":
        block = "2" if block != "0" else ("L" if link == "x+" else "R")
    elif link[0] == "z":
        block = "Z" + block
    else:
        region = {"F": "S", "F'": "S'"}[region]
    return phase, block, region, part


def rank(link, key):
    return key[0], ORDER[link[0]].index(key[2]), NEAR[key[1][-1]], key[3]


def plan(toks, cols, tasks):
    link_rate, pair_rate, hop, pair_hop, issue, ahead = 43e3, 500e3, 3.0, 1.5, 0.03, 5.0
    now, tick = 0.0, 0
    busy = dict.fromkeys(LINKS + ("pair",), 0.0)
    busy["pair"] = 3.2
    queue = {link: [] for link in LINKS}
    coming, have, steps = [], set(), []
    tasks = list(tasks)

    def post(when, what):
        nonlocal tick
        tick += 1
        heapq.heappush(coming, (when, tick, what))

    def size(key):
        return 2 * toks[key[0]] * cols[key[0]][key[2]]

    def pump():
        nonlocal now
        for link in LINKS:
            while queue[link] and busy[link] - now < ahead:
                key = min(queue[link], key=lambda k: rank(link, k))
                queue[link].remove(key)
                steps.append(("send", link, key))
                now += issue
                busy[link] = max(busy[link], now) + size(key) / link_rate
                post(busy[link] + hop, ("piece", landing(link, key)))

    def own(phase, part):
        for region in ORDER["x"]:
            for link in onward((phase, "0", region, part)):
                queue[link].append((phase, "0", region, part))

    for phase in range(len(toks)):
        own(phase, 0)
        post(1.6 + 0.5 * phase, ("own", phase))
    while True:
        while coming and coming[0][0] <= now:
            kind, key = heapq.heappop(coming)[2]
            if kind == "piece":
                have.add(("here", key))
                steps.append(("take", key))
                for link in onward(key):
                    queue[link].append(key)
                busy["pair"] = max(busy["pair"], now) + size(key) / pair_rate
                post(busy["pair"] + pair_hop, ("there", key))
                now += 2 * issue
            elif kind == "own":
                steps.append(("own", key))
                own(key, 1)
            else:
                have.add((kind, key))
            pump()
        pump()
        ready = [task for task in tasks if all(need in have for need in task[2])]
        if ready:
            name, took, _, reply = ready[0]
            tasks.remove(ready[0])
            steps.append(("task", name))
            now += took
            have.add(("done", name))
            if reply:
                post(now + reply, ("reply", name))
        elif coming:
            now = max(now, coming[0][0])
        else:
            break
    assert not tasks and not any(queue.values())
    return steps


def tiles_of(tok):
    return {64: (("0", "R"), ("2", "L")), 32: (("0", "R"), ("2", "L"))}[tok]


def make_tasks(toks, cols, grad_steps):
    tasks = []
    n = len(toks)
    for phase, tok in enumerate(toks):
        scale = tok / 32
        tasks.append((("merge1", phase), 0.2, (("reply", ("stats", phase)),), 4.5))
        tasks.append((("merge2", phase), 0.2, (("reply", ("merge1", phase)),), 0))
        tasks.append((("slope", phase), 0.1 + 0.3 * scale, (("done", ("merge2", phase)),), 0))
    for phase, tok in enumerate(toks):
        scale = tok / 32
        names = []
        for region in REGIONS:
            for tile in tiles_of(tok):
                name = ("logits", phase, region, tile)
                keys = [
                    (phase, block, region, part)
                    for b in tile for block in (("Z0",) if b == "0" else (b, "Z" + b)) for part in (0, 1)
                ]
                needs = [("here", key) for key in keys] + [("there", key) for key in keys]
                took = 0.1 + 3.9 * scale * len(tile) / 4 * cols[phase][region] / (24 * LANES)
                tasks.append((name, took, tuple(needs), 0))
                names.append(("done", name))
        tasks.append((("stats", phase), 0.1 + 0.25 * scale, tuple(names), 5.0))
    for phase, tok in enumerate(toks[:-1]):
        for i in range(grad_steps):
            tasks.append((("grad", phase, i), 0.1 + 3.2 * tok / 32 / grad_steps, (("done", ("slope", phase)),), 0))
    return tasks


def rectangle(total, rows, cols):
    return next((a, total // a) for a in range(1, rows + 1) if total % a == 0 and total // a <= cols)


def remote(src, dst, send_sem, recv_sem, device):
    return pltpu.make_async_remote_copy(
        src_ref=src, dst_ref=dst, send_sem=send_sem, recv_sem=recv_sem, device_id=device, device_id_type=MESH)


def gather_head(hidden, labels, head_weight):
    depth, n_cols = head_weight.shape
    half = depth // 2
    unit = half // sum(SIZES[0])
    toks = TOKENS_OF
    n_phase = len(toks)
    offs = [sum(toks[:i]) for i in range(n_phase)]
    cols = [dict(zip(REGIONS, (unit * s for s in sizes))) for sizes in SIZES]
    starts = [{r: sum(c[o] for o in REGIONS[:i]) for i, r in enumerate(REGIONS)} for c in cols]
    grad_step = 1024
    foreign = BLOCKS[1:] + tuple("Z" + b for b in BLOCKS)
    keys = [(p, b, r, part) for p in range(n_phase) for b in foreign for r in REGIONS for part in (0, 1)]
    sem_of = {key: i for i, key in enumerate(keys)}
    groups = [(p, b, r) for p in range(n_phase) for b in BLOCKS for r in REGIONS]
    group_of = {g: i for i, g in enumerate(groups)}
    steps = plan(toks, cols, make_tasks(toks, cols, depth // grad_step))
    joined = []
    for step in steps:
        if step[0] == "task" and step[1][0] == "grad":
            _, phase, i = step[1]
            if joined and joined[-1][0] == "task" and joined[-1][1][:2] == ("grad", phase):
                joined[-1] = ("task", ("grad", phase, joined[-1][1][2], i))
                continue
            step = ("task", ("grad", phase, i, i))
        joined.append(step)
    steps = joined
    width = [max(4 * t, 256) if t == 16 else 4 * t for t in toks]
    n_block = [N_CTX * t // w for t, w in zip(toks, width)]
    n_row = [N_CTX * t // LANES for t in toks]

    def kernel(hid_hbm, lab_ref, w_hbm, grad, h_last, st_last, loss, *scratch):
        scratch = list(scratch)
        H = [scratch.pop(0) for _ in range(n_phase - 1)] + [h_last]
        ST = [scratch.pop(0) for _ in range(n_phase - 1)] + [st_last]
        LT = [scratch.pop(0) for _ in range(n_phase)]
        S1 = [scratch.pop(0) for _ in range(n_phase)]
        S2 = [scratch.pop(0) for _ in range(n_phase)]
        LP = [scratch.pop(0) for _ in range(n_phase)]
        LR = [scratch.pop(0) for _ in range(n_phase)]
        (W, LB, hid_sem, w_sem, recv, pair_recv, own_recv, rest_recv, send, own_send, st_send, st_recv, lb_send,
         lb_recv) = scratch
        ctx, voc = lax.axis_index("ctx"), lax.axis_index("vocab")
        core, zl, x = ctx % 2, (ctx // 2) % 2, ctx // 4
        zh, y = voc % 2, voc // 2
        q = y % 2

        def at(xx, zz, cc):
            return (xx * 2 + zz) * 2 + cc

        right, left, across = (x + 1) % 4, (x + 3) % 4, (x + 2) % 4
        zp, zm = (zh * 2 + zl + 1) % 4, (zh * 2 + zl + 3) % 4
        pair = (at(x, zl, 1 - core), voc)
        device = {
            "x+": (at(right, zl, core), voc),
            "x-": (at(left, zl, core), voc),
            "z+": (at(x, zp % 2, core), y * 2 + zp // 2),
            "z-": (at(x, zm % 2, core), y * 2 + zm // 2),
            "y+": (ctx, (voc + 2) % N_VOCAB),
            "y-": (ctx, (voc + 6) % N_VOCAB),
        }
        ctx_peers = [((ctx + i) % N_CTX, voc) for i in range(1, N_CTX)]
        voc_peers = [(ctx, (voc + i) % N_VOCAB) for i in range(1, N_VOCAB)]
        cross = (at(x, 1 - zl, core), y * 2 + 1 - zh)
        barrier = pltpu.get_barrier_semaphore()
        greeted = ctx_peers + voc_peers + [cross]
        for peer in greeted:
            pl.semaphore_signal(barrier, inc=1, device_id=peer, device_id_type=MESH)

        def own_rows(phase, which):
            return pl.ds(pl.multiple_of(at(x, zl, which) * toks[phase], 16), toks[phase])

        def load(phase):
            return pltpu.make_async_copy(
                hid_hbm.at[pl.ds(offs[phase], toks[phase]), :], H[phase].at[own_rows(phase, core), :],
                hid_sem.at[phase])

        for phase in range(n_phase):
            load(phase).start()
        w_load = pltpu.make_async_copy(w_hbm, W, w_sem)
        w_load.start()
        LB[ctx] = lab_ref[...]
        xs = {"0": x, "L": left, "R": right, "2": across}

        def region_at(phase, region, which):
            ahead = starts[phase][region]
            back = half - ahead - cols[phase][region]
            return pl.multiple_of(which * half + jnp.where(q == 0, ahead, back), LANES)

        def piece(key):
            phase, block, region, part = key
            xb = xs[block[-1]]
            zb = 1 - zl if block[0] == "Z" else zl
            row = at(xb, zb, 1 - core if part else core) * toks[phase]
            return H[phase].at[
                pl.ds(pl.multiple_of(row, 16), toks[phase]),
                pl.ds(region_at(phase, region, core), cols[phase][region])]

        def link_copy(link, key):
            ref = piece(key)
            return remote(ref, ref, send.at[key[0], LINKS.index(link)], recv.at[sem_of[landing(link, key)]],
                          device[link])

        def take(key):
            ref = piece(key)
            phase, block, region, _ = key
            remote(ref, ref, send.at[phase, 6], recv.at[sem_of[key]], pair).wait_recv()
            remote(ref, ref, send.at[phase, 6], pair_recv.at[group_of[(phase, block[-1], region)]], pair).start()

        def drain(phase, a, b, sem):
            ref = H[phase].at[pl.ds(0, a), pl.ds(0, b)]
            return remote(ref, ref, sem, sem, pair)

        def own_copy(phase, theirs):
            first = pl.multiple_of((1 - core if theirs else core) * half, LANES)
            ref = H[phase].at[own_rows(phase, core), pl.ds(first, half)]
            return remote(ref, ref, own_send.at[phase], (own_recv if theirs else rest_recv).at[phase], pair)

        def stat_copy(buf, phase, index, stage, peer):
            ref = buf[phase].at[index]
            return remote(ref, ref, st_send.at[phase, stage], st_recv.at[phase, stage], peer)

        def stat_all(buf, phase, stage, n):
            ref = buf[phase].at[pl.ds(0, n - 1)]
            return remote(ref, ref, st_send.at[phase, stage], st_recv.at[phase, stage], pair)

        def label_all():
            ref = LB.at[pl.ds(0, N_CTX - 1)]
            return remote(ref, ref, lb_send, lb_recv, pair)

        for phase in range(n_phase):
            load(phase).wait()
        pl.semaphore_wait(barrier, len(greeted))
        for phase in range(n_phase):
            own_copy(phase, True).start()
            own_copy(phase, False).start()

        first_col = (ctx * N_VOCAB + voc) * n_cols
        seen = set()

        def once(*what):
            new = what not in seen
            seen.add(what)
            return new

        def block_rows(phase, xb):
            n = 4 * toks[phase]
            return pl.ds(pl.multiple_of(xb * n, n), n)

        def logits_task(phase, region, tile):
            if once("w"):
                w_load.wait()
            for b in tile:
                if once("group", phase, b, region):
                    n = toks[phase] * (2 if b == "0" else 4)
                    drain(phase, n, cols[phase][region], pair_recv.at[group_of[(phase, b, region)]]).wait_recv()
                if b == "0" and once("rest", phase):
                    drain(phase, toks[phase], half, rest_recv.at[phase]).wait_recv()
            spans = [pl.ds(region_at(phase, region, which), cols[phase][region]) for which in (core, 1 - core)]
            left_side = jnp.concatenate([W[k, :] for k in spans], axis=0)

            def product(blocks):
                rows = [block_rows(phase, xb) for xb in blocks]
                right_side = jnp.concatenate(
                    [jnp.concatenate([H[phase][r, k] for k in spans], axis=1) for r in rows], axis=0)
                part = lax.dot_general(
                    left_side, right_side, (((0,), (1,)), ((), ())), preferred_element_type=jnp.float32)
                for i, xb in enumerate(blocks):
                    piece_of = part[:, i * width[phase]:(i + 1) * width[phase]]
                    if region == REGIONS[0]:
                        LT[phase][xb] = piece_of
                    else:
                        LT[phase][xb] += piece_of

            if toks[phase] == 64:
                first = BLOCKS.index(tile[0])
                pl.loop(first, first + 2)(lambda i: product([lax.rem(x + i, N_X)]))
            else:
                product([xs[b] for b in tile])

        def label_mask(phase, i):
            ids = lax.broadcasted_iota(jnp.int32, (n_cols, width[phase]), 0)
            return ids == LR[phase][i] - first_col

        def label_rows():
            label_all().wait_recv()
            for phase, tok in enumerate(toks):
                per = width[phase] // tok
                for i in range(n_block[phase]):
                    LR[phase][i] = jnp.concatenate(
                        [LB[i * per + j][:, offs[phase]:offs[phase] + tok] for j in range(per)], axis=1)

        def stats_task(phase):
            if once("labels"):
                label_rows()
            per = width[phase] // LANES
            for i in range(n_block[phase]):
                lt = LT[phase][i]
                top = jnp.max(lt, axis=0, keepdims=True)
                total = jnp.sum(jnp.exp(lt - top), axis=0, keepdims=True)
                label = jnp.sum(jnp.where(label_mask(phase, i), lt, 0.0), axis=0, keepdims=True)
                for k, row in enumerate((top, total, label)):
                    for j in range(per):
                        r = i * per + j
                        S1[phase][ctx, k, r:r + 1, :] = row[:, j * LANES:(j + 1) * LANES]
            for peer in ctx_peers:
                stat_copy(S1, phase, ctx, 0, peer).start()

        def merged(buf, n):
            tops = [buf[i, 0] for i in range(n)]
            top = tops[0]
            for t in tops[1:]:
                top = jnp.maximum(top, t)
            total = sum(buf[i, 1] * jnp.exp(tops[i] - top) for i in range(n))
            return top, total, sum(buf[i, 2] for i in range(n))

        def merge1_task(phase):
            stat_all(S1, phase, 0, N_CTX).wait_recv()
            for k, row in enumerate(merged(S1[phase], N_CTX)):
                S2[phase][voc, k] = row
            for peer in voc_peers:
                stat_copy(S2, phase, voc, 1, peer).start()

        def merge2_task(phase):
            stat_all(S2, phase, 1, N_VOCAB).wait_recv()
            top, total, label = merged(S2[phase], N_VOCAB)
            lp = top + jnp.log(total)
            LP[phase][0] = lp
            LP[phase][1] = lp - label + z_weight * lp * lp
            first = ctx * toks[phase]
            row = LP[phase][1, pl.ds(first // LANES, 1), :]
            row = pltpu.roll(row, (offs[phase] - first % LANES + LANES) % LANES, 1)
            lane = lax.broadcasted_iota(jnp.int32, (1, LANES), 1)
            mine = (lane >= offs[phase]) & (lane < offs[phase] + toks[phase])
            loss[...] = jnp.where(mine, row, loss[...])

        def slope_task(phase):
            per = width[phase] // LANES
            for i in range(n_block[phase]):
                lp = jnp.concatenate([LP[phase][0, i * per + j:i * per + j + 1, :] for j in range(per)], axis=1)
                soft = jnp.exp(LT[phase][i] - lp)
                hot = jnp.where(label_mask(phase, i), 1.0, 0.0)
                ST[phase][:, i * width[phase]:(i + 1) * width[phase]] = (
                    (1.0 + 2.0 * z_weight * lp) * soft - hot).astype(jnp.bfloat16)

        def grad_run(phase, first, last):
            if first == last:
                grad_task(phase, first)
            else:
                pl.loop(first, last + 1)(lambda i: grad_task(phase, i))

        def grad_task(phase, i):
            rs = pl.ds(i * grad_step if isinstance(i, int) else pl.multiple_of(i * grad_step, grad_step), grad_step)
            part = lax.dot_general(
                H[phase][:, rs], ST[phase][...], (((0,), (1,)), ((), ())), preferred_element_type=jnp.float32)
            if phase == 0:
                grad[rs, :] = part
            else:
                grad[rs, :] += part

        run = {"logits": logits_task, "stats": stats_task, "merge1": merge1_task, "merge2": merge2_task,
               "slope": slope_task, "grad": grad_run}
        loss[...] = jnp.zeros_like(loss)
        for step in steps:
            if step[0] == "send":
                link_copy(step[1], step[2]).start()
            elif step[0] == "take":
                take(step[1])
            elif step[0] == "own":
                drain(step[1], toks[step[1]], half, own_recv.at[step[1]]).wait_recv()
                if step[1] == 0:
                    for peer in ctx_peers:
                        remote(LB.at[ctx], LB.at[ctx], lb_send, lb_recv, peer).start()
            else:
                run[step[1][0]](*step[1][1:])

        for phase in range(n_phase):
            for i, link in enumerate(LINKS):
                total = sum(cols[phase][s[2][2]] // unit for s in steps
                            if s[0] == "send" and s[1] == link and s[2][0] == phase)
                a, b = rectangle(total, N_CTX, depth // unit)
                drain(phase, a * toks[phase], b * unit, send.at[phase, i]).wait_send()
            drain(phase, 14 * toks[phase], half, send.at[phase, 6]).wait_send()
            drain(phase, toks[phase], depth, own_send.at[phase]).wait_send()
            stat_all(S1, phase, 0, N_CTX).wait_send()
            stat_all(S2, phase, 1, N_VOCAB).wait_send()
        label_all().wait_send()

    bf16, f32, i32 = jnp.bfloat16, jnp.float32, jnp.int32
    dma = pltpu.SemaphoreType.DMA
    vmem = pl.BlockSpec(memory_space=pltpu.VMEM)
    tokens = [N_CTX * t for t in toks]
    return pl.pallas_call(
        kernel,
        name="gather_head",
        out_shape=(pltpu.VMEM((depth, n_cols), f32), pltpu.VMEM((tokens[-1], depth), bf16),
                   pltpu.VMEM((n_cols, tokens[-1]), bf16), pltpu.VMEM((1, LANES), f32)),
        in_specs=[pl.BlockSpec(memory_space=pl.ANY), vmem, pl.BlockSpec(memory_space=pl.ANY)],
        out_specs=(vmem,) * 4,
        scratch_shapes=[
            *(pltpu.VMEM((n, depth), bf16) for n in tokens[:-1]),
            *(pltpu.VMEM((n_cols, n), bf16) for n in tokens[:-1]),
            *(pltpu.VMEM((n, n_cols, w), f32) for n, w in zip(n_block, width)),
            *(pltpu.VMEM((N_CTX, 3, n, LANES), f32) for n in n_row),
            *(pltpu.VMEM((N_VOCAB, 3, n, LANES), f32) for n in n_row),
            *(pltpu.VMEM((2, n, LANES), f32) for n in n_row),
            *(pltpu.VMEM((n, 1, w), i32) for n, w in zip(n_block, width)),
            pltpu.VMEM((depth, n_cols), bf16),
            pltpu.VMEM((N_CTX, 1, LANES), i32),
            dma((n_phase,)), dma, dma((len(keys),)), dma((len(groups),)), dma((n_phase,)), dma((n_phase,)),
            dma((n_phase, 7)), dma((n_phase,)), dma((n_phase, 2)), dma((n_phase, 2)), dma, dma,
        ],
        compiler_params=pltpu.CompilerParams(
            collective_id=0, has_side_effects=True, vmem_limit_bytes=42 * 2**20),
    )(hidden, labels.reshape(1, LANES), head_weight)


def finish(grad, h_last, st_last, loss):
    depth, n_cols = grad.shape
    step, slots = 1024, 3
    n = depth // step

    def kernel(grad_ref, h_ref, st_ref, loss_ref, out, loss_out, buf, sem):
        def copy(i):
            k = lax.rem(i, slots)
            return pltpu.make_async_copy(
                buf.at[k], out.at[pl.ds(pl.multiple_of(i * step, step), step), :], sem.at[k])

        loss_out[...] = loss_ref[...]

        @pl.loop(0, n)
        def _(i):
            @pl.when(i >= slots)
            def _():
                copy(i).wait()

            rs = pl.ds(pl.multiple_of(i * step, step), step)
            buf[lax.rem(i, slots)] = grad_ref[rs, :] + lax.dot_general(
                h_ref[:, rs], st_ref[...], (((0,), (1,)), ((), ())), preferred_element_type=jnp.float32)
            copy(i).start()

        for i in range(max(0, n - slots), n):
            copy(i).wait()

    vmem = pl.BlockSpec(memory_space=pltpu.VMEM)
    return pl.pallas_call(
        kernel,
        name="finish",
        out_shape=(jax.ShapeDtypeStruct((depth, n_cols), jnp.float32), jax.ShapeDtypeStruct((1, LANES), jnp.float32)),
        in_specs=[vmem] * 4,
        out_specs=(pl.BlockSpec(memory_space=pl.ANY), vmem),
        scratch_shapes=[pltpu.VMEM((slots, step, n_cols), jnp.float32), pltpu.SemaphoreType.DMA((slots,))],
        compiler_params=pltpu.CompilerParams(vmem_limit_bytes=16 * 2**20),
    )(grad, h_last, st_last, loss)


def head(hidden, labels, head_weight):
    parts = gather_head(hidden, labels, head_weight)
    parts = [pltpu.with_memory_space_constraint(p, pltpu.VMEM) for p in parts]
    grad, loss = finish(*parts)
    return loss.reshape(labels.shape), grad


def solution(mesh):
    return jax.shard_map(
        head,
        mesh=mesh,
        in_specs=(P("ctx", None), P("ctx"), P(None, ("ctx", "vocab"))),
        out_specs=(P("ctx"), P(None, ("ctx", "vocab"))),
        check_vma=False,
    )
```

profile of v0, /device:TPU:1, one launch (start us, length us, event | category | flops | bytes accessed | tf_op | source)
XLA Modules:
  0.0 88.9 jit_solution(12973222695632404540)
XLA Ops:
  0.6 81.7 %gather_head.1 = (f32[6144,512]{1,0:T(8,128)S(1)}, bf16[512,6144]{1,0:T(8,128)(2,1)S(1)}, bf16[512,512]{1,0:T(8,128)(2,1)S(1)}, f32[1,128]{1,0:T(1,128)S(1)}) custom-call(bf16[128,6144]{1,0:T(8,128)(2,1)} %hid_hbm.1, s32[1,128]{1,0:T(1,128)} %bitcast.2, bf16[6144,512]{1,0:T(8,128)(2,1)} %w_hbm.1), custom_call_target="tpu_custom_call" | custom-call | tf_op jit(solution)/shard_map/gather_head/pallas_call | solution.py:462
  82.4 6.4 %finish.1 = (f32[6144,512]{1,0:T(8,128)}, f32[1,128]{1,0:T(1,128)}) custom-call(f32[6144,512]{1,0:T(8,128)S(1)} %get-tuple-element.8.grad_ref, bf16[512,6144]{1,0:T(8,128)(2,1)S(1)} %get-tuple-element.9.h_ref, bf16[512,512]{1,0:T(8,128)(2,1)S(1)} %get-tuple-element.10.st_ref, f32[1,128]{1,0:T(1,128)S(1)} %get-tuple-element.11.loss_ref), custom_call_target="tpu_custom_call" | custom-call | tf_op jit(solution)/shard_map/finish/pallas_call | solution.py:515
where the time goes:
time: 89.1 us; the launch traced here: 88.9 us
  Pallas kernels  88.1 us (99%)
    pallas_call x1, Pallas kernels, gather_head(): pl.pallas_call(kernel, name='gather_head', out_shape=(pltpu.VMEM((depth,...  81.7 us
    pallas_call x1, Pallas kernels, finish(): pl.pallas_call(kernel, name='finish', out_shape=(jax.ShapeDtypeStruct((de...  6.35 us

commit v1 on v0

--- a/solution.py
+++ b/solution.py
@@ -56,7 +56,7 @@
 
 
 def plan(toks, cols, tasks):
-    link_rate, pair_rate, hop, pair_hop, issue, ahead = 43e3, 500e3, 3.0, 1.5, 0.03, 5.0
+    link_rate, pair_rate, hop, pair_hop, issue, ahead = 44e3, 500e3, 2.6, 1.5, 0.03, 3.5
     now, tick = 0.0, 0
     busy = dict.fromkeys(LINKS + ("pair",), 0.0)
     busy["pair"] = 3.2

time: 89.1 us -> 88.1 us (0.989)
  Pallas kernels: 88.1 us -> 87.1 us
    pallas_call x1, Pallas kernels: 81.7 us -> 80.8 us  [gather_head(): pl.pallas_call(kernel, name='gather_head', out_shape=(pltpu.VMEM((depth,...]
where the time goes in v1:
time: 88.1 us; the launch traced here: 88 us
  Pallas kernels  87.1 us (99%)
    pallas_call x1, Pallas kernels, gather_head(): pl.pallas_call(kernel, name='gather_head', out_shape=(pltpu.VMEM((depth,...  80.8 us
    pallas_call x1, Pallas kernels, finish(): pl.pallas_call(kernel, name='finish', out_shape=(jax.ShapeDtypeStruct((de...  6.36 us

profile of v1, /device:TPU:1, one launch (start us, length us, event | category | flops | bytes accessed | tf_op | source)
XLA Modules:
  0.0 88.0 jit_solution(18297002746157331991)
XLA Ops:
  0.6 80.8 %gather_head.1 = (f32[6144,512]{1,0:T(8,128)S(1)}, bf16[512,6144]{1,0:T(8,128)(2,1)S(1)}, bf16[512,512]{1,0:T(8,128)(2,1)S(1)}, f32[1,128]{1,0:T(1,128)S(1)}) custom-call(bf16[128,6144]{1,0:T(8,128)(2,1)} %hid_hbm.1, s32[1,128]{1,0:T(1,128)} %bitcast.2, bf16[6144,512]{1,0:T(8,128)(2,1)} %w_hbm.1), custom_call_target="tpu_custom_call" | custom-call | tf_op jit(solution)/shard_map/gather_head/pallas_call | solution.py:462
  81.4 6.4 %finish.1 = (f32[6144,512]{1,0:T(8,128)}, f32[1,128]{1,0:T(1,128)}) custom-call(f32[6144,512]{1,0:T(8,128)S(1)} %get-tuple-element.8.grad_ref, bf16[512,6144]{1,0:T(8,128)(2,1)S(1)} %get-tuple-element.9.h_ref, bf16[512,512]{1,0:T(8,128)(2,1)S(1)} %get-tuple-element.10.st_ref, f32[1,128]{1,0:T(1,128)S(1)} %get-tuple-element.11.loss_ref), custom_call_target="tpu_custom_call" | custom-call | tf_op jit(solution)/shard_map/finish/pallas_call | solution.py:515

commit v2 on v1

--- a/solution.py
+++ b/solution.py
@@ -247,7 +247,6 @@
         for phase in range(n_phase):
             load(phase).start()
         w_load = pltpu.make_async_copy(w_hbm, W, w_sem)
-        w_load.start()
         LB[ctx] = lab_ref[...]
         xs = {"0": x, "L": left, "R": right, "2": across}
 
@@ -299,6 +298,7 @@
 
         for phase in range(n_phase):
             load(phase).wait()
+        w_load.start()
         pl.semaphore_wait(barrier, len(greeted))
         for phase in range(n_phase):
             own_copy(phase, True).start()

time: 88.1 us -> 88.1 us (level)
  no operation moved by 1% of the time
where the time goes in v2:
time: 88.1 us; the launch traced here: 88 us
  Pallas kernels  87.1 us (99%)
    pallas_call x1, Pallas kernels, gather_head(): pl.pallas_call(kernel, name='gather_head', out_shape=(pltpu.VMEM((depth,...  80.8 us
    pallas_call x1, Pallas kernels, finish(): pl.pallas_call(kernel, name='finish', out_shape=(jax.ShapeDtypeStruct((de...  6.36 us

profile of v2, /device:TPU:1, one launch (start us, length us, event | category | flops | bytes accessed | tf_op | source)
XLA Modules:
  0.0 88.0 jit_solution(4058512861447859683)
XLA Ops:
  0.6 80.8 %gather_head.1 = (f32[6144,512]{1,0:T(8,128)S(1)}, bf16[512,6144]{1,0:T(8,128)(2,1)S(1)}, bf16[512,512]{1,0:T(8,128)(2,1)S(1)}, f32[1,128]{1,0:T(1,128)S(1)}) custom-call(bf16[128,6144]{1,0:T(8,128)(2,1)} %hid_hbm.1, s32[1,128]{1,0:T(1,128)} %bitcast.2, bf16[6144,512]{1,0:T(8,128)(2,1)} %w_hbm.1), custom_call_target="tpu_custom_call" | custom-call | tf_op jit(solution)/shard_map/gather_head/pallas_call | solution.py:462
  81.4 6.4 %finish.1 = (f32[6144,512]{1,0:T(8,128)}, f32[1,128]{1,0:T(1,128)}) custom-call(f32[6144,512]{1,0:T(8,128)S(1)} %get-tuple-element.8.grad_ref, bf16[512,6144]{1,0:T(8,128)(2,1)S(1)} %get-tuple-element.9.h_ref, bf16[512,512]{1,0:T(8,128)(2,1)S(1)} %get-tuple-element.10.st_ref, f32[1,128]{1,0:T(1,128)S(1)} %get-tuple-element.11.loss_ref), custom_call_target="tpu_custom_call" | custom-call | tf_op jit(solution)/shard_map/finish/pallas_call | solution.py:515
